TPU v7x, 32 devices: a whole 2x2x4 slice. The times are simulated.
32 devices in a mesh: leaf: 4 (over y, x), blk: 8 (over z, core).
Axes of the slice: x: 2, y: 2, z: 4, core: 2. Of those that a mesh axis runs over, the one named last changes fastest.
Arguments:
- near_tiles: bfloat16 [32, 8, 512, 512], P('leaf', 'blk'), may hold values from -0.25 to 0.25
- near_cols: int32 [32, 8], P('leaf', 'blk'), may hold values from 0 to 31, as said below
- near_count: int32 [32], P('leaf'), may hold values from 1 to 8, as said below
- probes: bfloat16 [32, 512, 512], P('leaf'), may hold values from -6 to 6
- mixing: float32 [512, 64], replicated, may hold values from -0.25 to 0.25
- far_tiles: bfloat16 [32, 8, 512, 512], P('leaf', 'blk'), may hold values from -6 to 6
- far_cols: int32 [32, 8], P('leaf', 'blk'), may hold values from 0 to 31, as said below
Outputs:
- coupling: float32 [32, 8, 64, 64], P('leaf', 'blk')
- root_part: float32 [32, 64, 64], P('leaf')
Inputs may be any that keep to these rules, and one draw needn't show every extreme that they name: near_cols[r, k] lies within 8 of r; the slots below near_count[r] name distinct clusters. Slots at or past near_count[r] hold arbitrary tiles that must be ignored. far_cols[r, j] differs from r by more than 8.
All inputs are finite; a program needn't handle non-finite values.
Results may differ from a plain program's by a relative error of at most 0.0041.
Values may be sent and summed in bfloat16 or wider, within the bound.
A program may use at most 128 MiB of HBM per device.

v0:
```python
import math

import jax
import jax.numpy as jnp
from jax import lax
from jax.sharding import PartitionSpec as P

RANK = 64
REACH = 8


highest = lax.Precision.HIGHEST


def padded(value, sides, width):
    for axis, dim in sides:
        peers, length = (lax.axis_size(axis), value.shape[dim])
        up = [(i, (i + 1) % peers) for i in range(peers - 1)]
        down = [(j, i) for i, j in up]
        last = lax.slice_in_dim(value, length - width, length, axis=dim)
        leading = lax.slice_in_dim(value, 0, width, axis=dim)
        before = lax.ppermute(last, axis, up)
        after = lax.ppermute(leading, axis, down)
        value = jnp.concatenate([before, value, after], axis=dim)
    return value


def partner_2(block, axis, apart):
    count = lax.axis_size(axis)
    route = []
    for low in range(count):
        high = low | 1 << apart
        if high != low and high < count:
            route += [(low, high), (high, low)]
    return lax.ppermute(block, axis, route)


def basis_from(gram_matrix, mixed_rows):
    lower_factor = jnp.linalg.cholesky(gram_matrix)
    solved = jax.scipy.linalg.solve_triangular(
        lower_factor, jnp.swapaxes(mixed_rows, -1, -2), lower=True
    )
    return jnp.swapaxes(solved, -1, -2)


def merge(stacked, mixing):
    mixed_rows = jnp.einsum("...mp,pk->...mk", stacked, mixing, precision=highest)
    gram_matrix = jnp.einsum("...mk,...ml->...kl", mixed_rows, mixed_rows, precision=highest)
    transfer = basis_from(gram_matrix, mixed_rows)
    merged = jnp.einsum("...mk,...mp->...kp", transfer, stacked, precision=highest)
    return (transfer, merged)


def shards(near_tiles, near_cols, near_count, probes, mixing, far_tiles, far_cols):
    local_rows = probes.shape[0]
    near_dev = near_tiles.shape[1]
    leaf_pos = lax.axis_index("leaf")
    blk_pos = lax.axis_index("blk")
    subtrees = lax.axis_size("leaf")
    clusters = local_rows * subtrees
    first_cluster = leaf_pos * local_rows - REACH
    window = padded(probes, (("leaf", 0),), REACH)

    def leaf_sketch(row_index):
        running = jnp.zeros((probes.shape[1], probes.shape[2]), jnp.float32)
        column = near_cols[row_index, 0] - first_cluster
        probe_block = lax.dynamic_index_in_dim(window, column, 0, keepdims=False)
        near_tile = near_tiles[row_index, 0]
        is_live = blk_pos * near_dev + 0 < near_count[row_index]
        running = lax.cond(
            is_live,
            lambda current: jnp.dot(near_tile, probe_block, preferred_element_type=jnp.float32),
            lambda current: current,
            running,
        )
        return running

    partial_sketch = lax.map(leaf_sketch, jnp.arange(local_rows))
    mixed_part = jnp.einsum("rbp,pk->rbk", partial_sketch, mixing, precision=highest)
    mixed_rows = lax.psum(mixed_part, "blk")
    gram_matrix = jnp.einsum("rbk,rbl->rkl", mixed_rows, mixed_rows, precision=highest)
    leaf_basis = basis_from(gram_matrix, mixed_rows)
    proj_part = jnp.einsum("rbk,rbp->rkp", leaf_basis, partial_sketch, precision=highest)
    leaf_proj = lax.psum(proj_part, "blk")
    basis_low = leaf_basis.astype(jnp.bfloat16)
    all_bases = lax.all_gather(basis_low, "leaf", axis=0, tiled=True)
    far_basis = all_bases[far_cols]
    far_image = jnp.einsum(
        "rjab,rjbk->rjak", far_tiles, far_basis, preferred_element_type=jnp.float32
    )
    coupling = jnp.einsum(
        "rak,rjal->rjkl", basis_low.astype(jnp.float32), far_image, precision=highest
    )
    sub_stack = leaf_proj.reshape(local_rows * RANK, leaf_proj.shape[2])
    sub_transfer, node_sketch = merge(sub_stack, mixing)
    levels = subtrees.bit_length() - 1
    path_factor = jnp.eye(RANK, dtype=jnp.float32)
    for depth_index in range(levels):
        partner = partner_2(node_sketch.astype(jnp.bfloat16), "leaf", depth_index).astype(
            node_sketch.dtype
        )
        is_upper = leaf_pos >> depth_index & 1
        lower_half = jnp.where(is_upper == 1, partner, node_sketch)
        upper_half = jnp.where(is_upper == 1, node_sketch, partner)
        transfer, node_sketch = merge(jnp.concatenate([lower_half, upper_half], 0), mixing)
        picked = lax.dynamic_slice_in_dim(transfer, is_upper * RANK, RANK, 0)
        path_factor = jnp.dot(path_factor, picked, precision=highest)
    sub_blocks = sub_transfer.reshape(local_rows, RANK, RANK)
    root_part = jnp.einsum("cab,bd->cad", sub_blocks, path_factor, precision=highest)
    root_part = root_part * math.sqrt(clusters * RANK)
    return (coupling, root_part)


def solution(mesh):
    in_specs = (
        P("leaf", "blk", None, None),
        P("leaf", "blk"),
        P("leaf"),
        P("leaf", None, None),
        P(),
        P("leaf", "blk", None, None),
        P("leaf", "blk"),
    )
    out_specs = (P("leaf", "blk", None, None), P("leaf", None, None))
    return jax.shard_map(shards, mesh=mesh, in_specs=in_specs, out_specs=out_specs, check_vma=False)
```

profile of v0, /device:TPU:25, one launch (start us, length us, event | category | flops | bytes accessed | tf_op | source)
XLA Modules:
  0.0 556.9 jit_solution(8222084154776121262)
XLA Ops:
  7.2 5.1 collective-permute-start
  12.3 1.3 collective-permute-start.1
  13.7 86.2 %collective-permute-done = bf16[8,512,512]{2,1,0:T(8,128)(2,1)} collective-permute-done((bf16[8,512,512]{2,1,0:T(8,128)(2,1)}, bf16[8,512,512]{2,1,0:T(8,128)(2,1)}, u32[]{:S(2)}, u32[]{:S(2)}) %collective-permute-start) | collective-permute-done | bytes 4194336 | tf_op jit(solution)/shard_map/ppermute | solution.py:22
  99.9 91.8 %collective-permute-done.1 = bf16[8,512,512]{2,1,0:T(8,128)(2,1)} collective-permute-done((bf16[8,512,512]{2,1,0:T(8,128)(2,1)}, bf16[8,512,512]{2,1,0:T(8,128)(2,1)}, u32[]{:S(2)}, u32[]{:S(2)}) %collective-permute-start.1) | collective-permute-done | bytes 4194336 | tf_op jit(solution)/shard_map/ppermute | solution.py:23
  191.7 10.8 %pad_maximum_fusion = bf16[24,512,512]{2,1,0:T(8,128)(2,1)} fusion(bf16[8,512,512]{2,1,0:T(8,128)(2,1)} %collective-permute-done.1, bf16[8,512,512]{2,1,0:T(8,128)(2,1)} %param.17, bf16[8,512,512]{2,1,0:T(8,128)(2,1)} %collective-permute-done), kind=kLoop, calls=%fused_computation.9 | loop fusion | flops 12582912 | bytes 25165824 | tf_op jit(solution)/shard_map/concatenate | solution.py:24
  202.5 39.0 %while.10 = (s32[]{:T(128)}, f32[8,512,512]{2,1,0:T(8,128)}, s32[8]{0:T(128)S(1)}, s32[8]{0:T(128)S(1)}, s32[]{:T(128)}, /*index=5*/bf16[8,1,512,512]{3,2,1,0:T(...) while((s32[]{:T(128)}, f32[8,512,512]{2,1,0:T(8,128)}, ...), condition=%wide.region_3.4_spmd, body=%wide.region_0.3_spmd.sunk | while | flops 268435456 | bytes 4195627 | solution.py:78
  202.5 0.6 dynamic_slice.44
  204.9 0.6 dynamic_slice.45
  206.3 1.1 constant_dynamic-update-slice_fusion.2
  207.4 0.6 dynamic_slice.44
  209.9 0.6 dynamic_slice.45
  211.2 1.0 constant_dynamic-update-slice_fusion.2
  212.3 0.6 dynamic_slice.44
  214.7 0.6 dynamic_slice.45
  216.1 1.1 constant_dynamic-update-slice_fusion.2
  217.1 0.6 dynamic_slice.44
  219.5 0.6 dynamic_slice.45
  220.9 1.1 constant_dynamic-update-slice_fusion.2
  222.0 0.6 dynamic_slice.44
  224.4 0.6 dynamic_slice.45
  225.8 1.1 constant_dynamic-update-slice_fusion.2
  226.8 0.6 dynamic_slice.44
  229.3 0.6 dynamic_slice.45
  230.6 1.1 constant_dynamic-update-slice_fusion.2
  231.7 0.6 dynamic_slice.44
  234.2 0.6 dynamic_slice.45
  235.5 1.1 constant_dynamic-update-slice_fusion.2
  236.6 0.6 dynamic_slice.44
  239.0 0.6 dynamic_slice.45
  240.4 1.1 constant_dynamic-update-slice_fusion.2
  241.5 11.5 %fusion.17 = f32[8,512,64]{1,2,0:T(8,128)} fusion(f32[8,512,512]{2,1,0:T(8,128)} %get-tuple-element.118, f32[512,64]{0,1:T(8,128)S(1)} %copy-done), kind=kOutput, calls=%fused_computation.34 | convolution fusion | flops 1610612736 | bytes 9568256 | tf_op jit(solution)/shard_map/rbp,pk->rbk/dot_general | solution.py:79
  253.1 75.4 %all-reduce.3.cloned.1.call-done = f32[8,512,64]{1,2,0:T(8,128)} async-done(((f32[8,512,64]{1,2,0:T(8,128)}), f32[8,512,64]{1,2,0:T(8,128)}) %all-reduce.3.cloned.1.call-update) | async-done | bytes 1048592 | tf_op jit(solution)/shard_map/psum | solution.py:80
  328.5 2.6 fusion.44
  331.3 46.9 %custom-call.17 = f32[8,64,64]{2,1,0:T(8,128)S(1)} custom-call(f32[8,64,64]{2,1,0:T(8,128)S(1)} %fusion.13), custom_call_target="Cholesky" | custom-call | tf_op jit(solution)/shard_map/jit(cholesky)/cholesky | solution.py:39
  378.5 39.3 %custom-call.18 = f32[8,1,64,64]{2,3,1,0:T(8,128)S(1)} custom-call(f32[8,1,64,64]{3,2,1,0:T(8,128)S(1)} %select_bitcast_fusion), custom_call_target="InvertDiagBlocksLowerTriangular" | custom-call | tf_op jit(solution)/shard_map/jit(_solve_triangular)/vmap()/triangular_solve | solution.py:40
  417.8 2.3 fusion.11
  420.1 8.5 %fusion.45 = f32[8,64,512]{2,1,0:T(8,128)} fusion(f32[8,64,512]{2,1,0:T(8,128)S(1)} %fusion.11, f32[8,512,512]{2,1,0:T(8,128)} %get-tuple-element.118), kind=kOutput, calls=%fused_computation.79 | convolution fusion | flops 1610612736 | bytes 10485760 | tf_op jit(solution)/shard_map/rbk,rbp->rkp/dot_general | solution.py:83
  428.9 57.7 %all-reduce.5.cloned.1.call-done = f32[512,512]{1,0:T(8,128)} async-done(((f32[512,512]{1,0:T(8,128)}), f32[512,512]{1,0:T(8,128)}) %all-reduce.5.cloned.1.call-update) | async-done | bytes 1048592 | tf_op jit(solution)/shard_map/psum | solution.py:84
  486.7 2.4 fusion.46
  489.4 5.8 %cholesky.97 = f32[64,64]{1,0:T(8,128)S(1)} custom-call(f32[64,64]{1,0:T(8,128)S(1)} %fusion.32), custom_call_target="Cholesky" | custom-call | tf_op jit(solution)/shard_map/jit(cholesky)/cholesky | solution.py:39
  495.3 0.6 compare_reduce_fusion.3
  495.9 0.7 fusion.19
  496.6 4.9 custom-call.19
  501.8 2.0 fusion.42
  503.8 1.2 collective-permute-start.2
  505.0 0.9 convert_bitcast_fusion
  506.1 0.9 collective-permute-done.2
  507.0 0.4 fusion.16
  507.7 5.8 %cholesky.108 = f32[64,64]{1,0:T(8,128)S(1)} custom-call(f32[64,64]{1,0:T(8,128)S(1)} %fusion.29), custom_call_target="Cholesky" | custom-call | tf_op jit(solution)/shard_map/jit(cholesky)/cholesky | solution.py:39
  513.6 0.6 compare_reduce_fusion.2
  514.2 0.7 fusion.20
  514.9 4.9 custom-call.21
  520.3 1.3 collective-permute-start.3
  521.8 2.5 collective-permute-done.3
  525.0 5.8 %cholesky.119 = f32[64,64]{1,0:T(8,128)S(1)} custom-call(f32[64,64]{1,0:T(8,128)S(1)} %fusion.25), custom_call_target="Cholesky" | custom-call | tf_op jit(solution)/shard_map/jit(cholesky)/cholesky | solution.py:39
  530.9 0.6 compare_reduce_fusion.1
  531.5 0.7 fusion.21
  532.2 4.9 custom-call.22
  537.6 1.1 convolution_multiply_fusion
  538.7 4.5 all-gather.2.cloned.1.call-done
  543.1 2.2 gather_fusion
  545.3 3.6 fusion.5
  548.9 0.6 convolution_bitcast_fusion.1
  549.5 0.8 copy.29
  (63 shorter events, 6.0 us)
Async XLA Ops:
  7.2 234.3 %copy-start = (f32[512,64]{0,1:T(8,128)S(1)}, f32[512,64]{0,1:T(8,128)}, u32[]{:S(2)}) copy-start(f32[512,64]{0,1:T(8,128)} %param.18) | copy-start | bytes 393220
  7.2 321.3 %all-reduce.3.cloned.1.call-start = ((), (), s32[]{:S(2)}) async-start(), calls=%async_computation | async-start | bytes 2097152 | tf_op jit(solution)/shard_map/psum | solution.py:80
  7.2 92.7 %collective-permute-start = (bf16[8,512,512]{2,1,0:T(8,128)(2,1)}, bf16[8,512,512]{2,1,0:T(8,128)(2,1)}, u32[]{:S(2)}, u32[]{:S(2)}) collective-permute-start(bf16[8,512,512]{2,1,0:T(8,128)(2,1)} %param.17), channel_id=1, source_target_pairs={{0,8},{8,16},{16,24},{1,9},{9,17},{17,25},{2,10},{10,18},{18,26},{... | collective-permute-start | bytes 12582920 | tf_op jit(solution)/shard_map/ppermute | solution.py:22
  12.3 179.4 %collective-permute-start.1 = (bf16[8,512,512]{2,1,0:T(8,128)(2,1)}, bf16[8,512,512]{2,1,0:T(8,128)(2,1)}, u32[]{:S(2)}, u32[]{:S(2)}) collective-permute-start(bf16[8,512,512]{2,1,0:T(8,128)(2,1)} %param.17), channel_id=1, source_target_pairs={{8,0},{16,8},{24,16},{9,1},{17,9},{25,17},{10,2},{18,10},{26,18},{... | collective-permute-start | bytes 12582920 | tf_op jit(solution)/shard_map/ppermute | solution.py:23
  13.6 188.8 %copy-start.1 = (s32[8]{0:T(128)S(1)}, s32[8]{0:T(128)}, u32[]{:S(2)}) copy-start(s32[8]{0:T(128)} %param.16) | copy-start | bytes 100
  13.6 188.8 %copy-start.2 = (s32[8,1]{0,1:T(1,128)S(1)}, s32[8,1]{0,1:T(1,128)}, u32[]{:S(2)}) copy-start(s32[8,1]{0,1:T(1,128)} %param.15) | copy-start | bytes 100
  253.0 233.6 %all-reduce.5.cloned.1.call-start = ((), (), s32[]{:S(2)}) async-start(), calls=%async_computation.2 | async-start | bytes 2097152 | tf_op jit(solution)/shard_map/psum | solution.py:84
  331.1 97.8 %copy-start.3 = (s32[8,1]{0,1:T(1,128)S(1)}, s32[8,1]{0,1:T(1,128)}, u32[]{:S(2)}) copy-start(s32[8,1]{0,1:T(1,128)} %param.20) | copy-start | bytes 100
  428.7 114.5 %all-gather.2.cloned.1.call-start = ((), (), s32[]{:S(2)}) async-start(), calls=%async_computation.1 | async-start | bytes 2621440 | tf_op jit(solution)/shard_map/all_gather | solution.py:86
  503.8 3.2 collective-permute-start.2
  520.3 4.0 collective-permute-start.3
Sparse Core Ops, SparseCore 0:
  253.1 75.3 all-reduce.2
  428.8 57.8 all-reduce.4
  506.0 37.0 all-gather.1
where the time goes:
time: 560 us; the launch traced here: 557 us
  waiting for transfers between devices  319 us (57%)
  other arithmetic  134 us (24%)
  matrix products  37.6 us (7%)
  local copies, waits for them, and re-layouts  22.5 us (4%)
  loops' own time  20 us (4%)
  between operations  14.1 us (3%)
  starting transfers between devices  9.18 us (2%)
    ppermute x1, waiting for transfers between devices, padded(): after = lax.ppermute(leading, axis, down)  91.8 us
    ppermute x1, waiting for transfers between devices, padded(): before = lax.ppermute(last, axis, up)  86.2 us
    psum x1, waiting for transfers between devices, shards(): mixed_rows = lax.psum(mixed_part, 'blk')  75.4 us
    another operation x13, other arithmetic, basis_from(): lower_factor = jnp.linalg.cholesky(gram_matrix)  66.6 us
    psum x1, waiting for transfers between devices, shards(): leaf_proj = lax.psum(proj_part, 'blk')  57.7 us
    another operation x9, other arithmetic, basis_from(): jax.scipy.linalg.solve_triangular(lower_factor, jnp.swapaxes(mixed_rows,...  56.1 us
    another operation x1, loops' own time, shards(): partial_sketch = lax.map(leaf_sketch, jnp.arange(local_rows))  19.9 us
    dot_general x1, matrix products, shards(): jnp.einsum('rbp,pk->rbk', partial_sketch, mixing, precision=highest)  11.5 us
  transfers between devices with their start and end apart: 7, of which 7 were waited for; matrix products, arithmetic and copies ran while one was open for 5% of the time, Pallas kernels for 0%

commit v1 on v0

v1 whole, which is shorter than its diff:
```python
import functools
import math

import jax
import jax.numpy as jnp
from jax import lax
from jax.experimental import pallas as pl
from jax.experimental.pallas import tpu as pltpu
from jax.sharding import PartitionSpec as P

REACH = 8
MESH = pl.DeviceIdType.MESH
highest = lax.Precision.HIGHEST
f32 = jnp.float32
bf16 = jnp.bfloat16


def split_terms(value):
    high = value.astype(bf16)
    low = (value - high.astype(f32)).astype(bf16)
    return jnp.concatenate([high, low], axis=1)


def factor(gram):
    rank = gram.shape[0]
    rows = lax.broadcasted_iota(jnp.int32, (rank, 2 * rank), 0)
    lanes = lax.broadcasted_iota(jnp.int32, (rank, 2 * rank), 1)
    unit = jnp.where(lanes - rank == rows, 1.0, 0.0).astype(f32)
    work = jnp.where(lanes < rank, jnp.concatenate([gram, gram], axis=1), unit)
    done = []
    for start in range(0, rank, 8):
        index = lax.broadcasted_iota(jnp.int32, work.shape, 0)
        for step in range(8):
            j = start + step
            row = work[step : step + 1, :]
            inverse = 1.0 / work[step : step + 1, j : j + 1]
            column = work[:, j : j + 1]
            work = work - jnp.where(index > step, column * (row * inverse), 0.0)
        done.append(work[:8])
        work = work[8:] if start + 8 < rank else None
    full = jnp.concatenate(done, axis=0)
    pivots = jnp.sum(jnp.where(lanes == rows, full, 0.0), axis=1, keepdims=True)
    full = full / jnp.sqrt(pivots)
    upper = jnp.where(lanes >= rows, full, 0.0)[:, :rank]
    return upper, full[:, rank:]


def kernel(
    nl, nb, scale,
    cols, count, fcols, near_hbm, probes_hbm, mix, far_hbm,
    coup, root,
    pv, nv, fv, ywin, part, pair, sums, scat, gbuf, gleaf, ubuf, ball,
    pin, win, h_s, h_r, f_s, f_r, p_s, p_r, r_s, r_r, g_s, g_r, gl_s, gl_r,
    u_s, u_r, bm_s, bm_r, bz_s, bz_r, bl_s, bl_r, bx_s, bx_r,
):
    leaf = lax.axis_index("leaf")
    blk = lax.axis_index("blk")
    R = pv.shape[0]
    half = R // 2
    nz = nb // 2
    groups = nb // R
    size = pv.shape[1]
    rank = mix.shape[1]
    near_dev = nv.shape[1]
    far_dev = fv.shape[1]
    core = blk % 2
    own = blk % R
    z = own // 2
    base = blk - own
    mate = blk + 1 - 2 * core
    pending = []

    def remote(src, dst, send, recv, to_leaf, to_blk):
        return pltpu.make_async_remote_copy(
            src_ref=src, dst_ref=dst, send_sem=send, recv_sem=recv,
            device_id=(to_leaf, to_blk), device_id_type=MESH,
        )

    loads = []
    for k in range(half):
        loads.append(pltpu.make_async_copy(probes_hbm.at[2 * k + core], pv.at[2 * k + core], pin.at[k]))
    for k in range(half):
        i = 2 * k + 1 - core
        loads.append(pltpu.make_async_copy(probes_hbm.at[i], pv.at[i], pin.at[half + k]))
    near_load = pltpu.make_async_copy(near_hbm, nv, win.at[0])
    far_load = pltpu.make_async_copy(far_hbm, fv, win.at[1])
    for load in loads:
        load.start()
    near_load.start()
    far_load.start()

    barrier = pltpu.get_barrier_semaphore()
    for d in range(1, nl):
        pl.semaphore_signal(barrier, inc=1, device_id=((leaf + d) % nl, blk), device_id_type=MESH)
    for d in range(1, nb):
        pl.semaphore_signal(barrier, inc=1, device_id=(leaf, (blk + d) % nb), device_id_type=MESH)

    terms = split_terms(mix[...])

    def mixed(i):
        product = jnp.dot(pv[i], terms, preferred_element_type=f32)
        ywin[R + i] = split_terms(product[:, :rank] + product[:, rank:])

    def up_copy(k):
        i = 2 * k + core
        return remote(ywin.at[R + i], ywin.at[i], h_s.at[k], h_r.at[k], (leaf + 1) % nl, blk)

    def down_copy(k):
        i = 2 * k + core
        return remote(
            ywin.at[R + i], ywin.at[2 * R + i], h_s.at[half + k], h_r.at[half + k], (leaf + nl - 1) % nl, blk
        )

    def share(side, k, parity):
        i = 2 * R * side + 2 * k + parity
        s = side * half + k
        return remote(ywin.at[i], ywin.at[i], f_s.at[s], f_r.at[s], leaf, mate)

    has_up = leaf < nl - 1
    has_down = leaf > 0
    for k in range(half):
        loads[k].wait()
        mixed(2 * k + core)
        if k == 0:
            pl.semaphore_wait(barrier, nl - 1 + nb - 1)

        @pl.when(has_up)
        def _():
            up_copy(k).start()

        @pl.when(has_down)
        def _():
            down_copy(k).start()

    for k in range(half):
        loads[half + k].wait()
        mixed(2 * k + 1 - core)

    @pl.when(jnp.logical_not(has_down))
    def _():
        ywin[0:R] = jnp.zeros((R,) + ywin.shape[1:], bf16)

    @pl.when(jnp.logical_not(has_up))
    def _():
        ywin[2 * R : 3 * R] = jnp.zeros((R,) + ywin.shape[1:], bf16)

    for k in range(half):

        @pl.when(has_down)
        def _():
            up_copy(k).wait_recv()
            share(0, k, core).start()

        @pl.when(has_up)
        def _():
            down_copy(k).wait_recv()
            share(1, k, core).start()

    for k in range(half):

        @pl.when(has_down)
        def _():
            share(0, k, 1 - core).wait_recv()

        @pl.when(has_up)
        def _():
            share(1, k, 1 - core).wait_recv()

    near_load.wait()

    def compressed(r):
        total = jnp.zeros((size, rank), f32)
        for s in range(near_dev):
            column = jnp.clip(cols[r, s] - (leaf - 1) * R, 0, 3 * R - 1)
            product = jnp.dot(nv[r, s], ywin[column], preferred_element_type=f32)
            live = blk * near_dev + s < count[r]
            total += jnp.where(live, product[:, :rank] + product[:, rank:], 0.0)
        return jnp.concatenate([total[: size // 2], total[size // 2 :]], axis=1)

    for k in range(half):
        part[k] = compressed(2 * k + 1 - core)
        copy = remote(part.at[k], pair.at[k], p_s.at[k], p_r.at[k], leaf, mate)
        copy.start()
        pending.append(copy)

    slot = blk // 2
    for k in range(half):
        mine = compressed(2 * k + core)
        pending[k].wait_recv()
        sums[k] = mine + pair[k]
        for g in range(groups):
            target = g * R + 2 * k + core

            @pl.when(target != blk)
            def _():
                remote(sums.at[k], scat.at[slot], r_s.at[k, g], r_r.at[slot], leaf, target).start()

            @pl.when(target == blk)
            def _():
                scat[slot] = sums[k]

    for d in range(1, nz):
        s = (slot + d) % nz
        remote(sums.at[0], scat.at[s], r_s.at[0, 0], r_r.at[s], leaf, mate).wait_recv()
    x = scat[0]
    for s in range(1, nz):
        x = x + scat[s]

    product = lax.dot_general(x, x, (((0,), (0,)), ((), ())), precision=highest, preferred_element_type=f32)
    gram = product[:rank, :rank] + product[rank:, rank:]
    gbuf[own] = gram
    for d in range(1, R):
        j = (own + d) % R
        copy = remote(gbuf.at[own], gbuf.at[own], g_s.at[d], g_r.at[own], leaf, base + j)
        copy.start()
        pending.append(copy)

    upper, inverse = factor(gram)
    zero = jnp.zeros((rank, rank), f32)
    twice = jnp.concatenate(
        [jnp.concatenate([inverse, zero], axis=1), jnp.concatenate([zero, inverse], axis=1)], axis=0
    )
    basis = lax.dot_general(x, twice, (((1,), (1,)), ((), ())), precision=highest, preferred_element_type=f32)

    def place(q_leaf, parity, q_z):
        return (q_leaf * 2 + parity) * half + q_z

    def spread(q_z):
        at = place(leaf, core, q_z)
        copies = [remote(ball.at[at], ball.at[at], bm_s.at[q_z], bm_r.at[q_z], leaf, mate)]
        for d in range(1, nl):
            copies.append(
                remote(
                    ball.at[at], ball.at[at], bl_s.at[d, q_z], bl_r.at[leaf, q_z], (leaf + d) % nl, blk
                )
            )
        for copy in copies:
            copy.start()
            pending.append(copy)

    at = place(leaf, core, z)
    ball[at] = basis.astype(bf16)
    for d in range(1, half):
        to = (z + d) % half
        copy = remote(ball.at[at], ball.at[at], bz_s.at[d], bz_r.at[z], leaf, base + 2 * to + core)
        copy.start()
        pending.append(copy)
    spread(z)
    ubuf[own] = upper
    for d in range(1, R):
        j = (own + d) % R
        copy = remote(ubuf.at[own], ubuf.at[own], u_s.at[d], u_r.at[own], leaf, base + j)
        copy.start()
        pending.append(copy)

    for d in range(1, R):
        j = (own + d) % R
        remote(gbuf.at[j], gbuf.at[j], g_s.at[d], g_r.at[j], leaf, mate).wait_recv()
    gram = gbuf[0]
    for j in range(1, R):
        gram = gram + gbuf[j]
    gleaf[leaf] = gram
    for d in range(1, nl):
        copy = remote(gleaf.at[leaf], gleaf.at[leaf], gl_s.at[d], gl_r.at[leaf], (leaf + d) % nl, blk)
        copy.start()
        pending.append(copy)

    for d in range(1, half):
        other = (z + d) % half
        at = place(leaf, core, other)
        remote(ball.at[at], ball.at[at], bz_s.at[d], bz_r.at[other], leaf, mate).wait_recv()
        spread(other)

    for d in range(1, nl):
        s = (leaf + d) % nl
        remote(gleaf.at[s], gleaf.at[s], gl_s.at[d], gl_r.at[s], s, blk).wait_recv()
    gram = gleaf[0]
    for s in range(1, nl):
        gram = gram + gleaf[s]
    _, root_inverse = factor(gram)

    for d in range(1, nl):
        s = (leaf + nl - d) % nl
        for k in range(half):
            at = place(s, core, k)
            remote(ball.at[at], ball.at[at], bl_s.at[d, k], bl_r.at[s, k], s, blk).wait_recv()
        span = pl.ds(place(s, core, 0), half)
        copy = remote(ball.at[span], ball.at[span], bx_s.at[d], bx_r.at[s], leaf, mate)
        copy.start()
        pending.append(copy)

    for d in range(1, R):
        j = (own + d) % R
        remote(ubuf.at[j], ubuf.at[j], u_s.at[d], u_r.at[j], leaf, mate).wait_recv()
    for r in range(R):
        root[r] = scale * lax.dot_general(
            ubuf[r], root_inverse, (((1,), (1,)), ((), ())), precision=highest, preferred_element_type=f32
        )

    for k in range(half):
        at = place(leaf, 1 - core, k)
        remote(ball.at[at], ball.at[at], bm_s.at[k], bm_r.at[k], leaf, mate).wait_recv()
    for d in range(1, nl):
        s = (leaf + nl - d) % nl
        span = pl.ds(place(s, 1 - core, 0), half)
        remote(ball.at[span], ball.at[span], bx_s.at[d], bx_r.at[s], leaf, mate).wait_recv()
    far_load.wait()

    def unpacked(block):
        return jnp.concatenate([block[:, :rank], block[:, rank:]], axis=0)

    for r in range(R):
        left = unpacked(ball[place(leaf, r % 2, r // 2)])
        for s in range(far_dev):
            q = fcols[r, s]
            right = unpacked(ball[place(q // R, q % 2, (q % R) // 2)])
            image = jnp.dot(fv[r, s], right, preferred_element_type=f32)
            product = lax.dot_general(
                left, split_terms(image), (((0,), (0,)), ((), ())), preferred_element_type=f32
            )
            coup[r, s] = product[:, :rank] + product[:, rank:]

    for copy in pending:
        copy.wait_send()
    for k in range(half):

        @pl.when(has_up)
        def _():
            up_copy(k).wait_send()
            share(1, k, core).wait_send()

        @pl.when(has_down)
        def _():
            down_copy(k).wait_send()
            share(0, k, core).wait_send()

        for g in range(groups):
            target = g * R + 2 * k + core

            @pl.when(target != blk)
            def _():
                remote(sums.at[k], scat.at[slot], r_s.at[k, g], r_r.at[slot], leaf, target).wait_send()


def shards(near_tiles, near_cols, near_count, probes, mixing, far_tiles, far_cols):
    nl, nb = lax.axis_size("leaf"), lax.axis_size("blk")
    R, size, width = probes.shape
    rank = mixing.shape[1]
    half, nz, groups = R // 2, nb // 2, nb // R
    assert R % 2 == 0 and nb % R == 0 and REACH <= R and nl > 1
    dma = pltpu.SemaphoreType.DMA
    packed = (size // 2, 2 * rank)
    vmem = pl.BlockSpec(memory_space=pltpu.VMEM)
    smem = pl.BlockSpec(memory_space=pltpu.SMEM)
    hbm = pl.BlockSpec(memory_space=pl.ANY)
    scale = math.sqrt(nl * R * rank)
    return pl.pallas_call(
        functools.partial(kernel, nl, nb, scale),
        out_shape=(
            jax.ShapeDtypeStruct((R, far_tiles.shape[1], rank, rank), f32),
            jax.ShapeDtypeStruct((R, rank, rank), f32),
        ),
        in_specs=[smem, smem, smem, hbm, hbm, vmem, hbm],
        out_specs=(vmem, vmem),
        scratch_shapes=[
            pltpu.VMEM(probes.shape, bf16),
            pltpu.VMEM(near_tiles.shape, bf16),
            pltpu.VMEM(far_tiles.shape, bf16),
            pltpu.VMEM((3 * R, size, 2 * rank), bf16),
            pltpu.VMEM((half,) + packed, f32),
            pltpu.VMEM((half,) + packed, f32),
            pltpu.VMEM((half,) + packed, f32),
            pltpu.VMEM((nz,) + packed, f32),
            pltpu.VMEM((R, rank, rank), f32),
            pltpu.VMEM((nl, rank, rank), f32),
            pltpu.VMEM((R, rank, rank), f32),
            pltpu.VMEM((nl * R,) + packed, bf16),
            dma((R,)), dma((2,)),
            dma((R,)), dma((R,)), dma((R,)), dma((R,)),
            dma((half,)), dma((half,)),
            dma((half, groups)), dma((nz,)),
            dma((R,)), dma((R,)), dma((nl,)), dma((nl,)),
            dma((R,)), dma((R,)), dma((half,)), dma((half,)),
            dma((half,)), dma((half,)),
            dma((nl, half)), dma((nl, half)), dma((nl,)), dma((nl,)),
        ],
        compiler_params=pltpu.CompilerParams(
            collective_id=0, has_side_effects=True, vmem_limit_bytes=48 * 1024 * 1024
        ),
        name="nested_basis",
    )(near_cols, near_count, far_cols, near_tiles, probes, mixing, far_tiles)


def solution(mesh):
    in_specs = (
        P("leaf", "blk", None, None),
        P("leaf", "blk"),
        P("leaf"),
        P("leaf", None, None),
        P(),
        P("leaf", "blk", None, None),
        P("leaf", "blk"),
    )
    out_specs = (P("leaf", "blk", None, None), P("leaf", None, None))
    return jax.shard_map(shards, mesh=mesh, in_specs=in_specs, out_specs=out_specs, check_vma=False)
```

time: 560 us -> 88.3 us (0.16)
  waiting for transfers between devices: 319 us -> 0 us
  other arithmetic: 134 us -> 0 us
  Pallas kernels: 0 us -> 80.7 us
  matrix products: 37.6 us -> 0 us
  loops' own time: 20 us -> 0 us
  local copies, waits for them, and re-layouts: 22.5 us -> 6.73 us
  between operations: 14.1 us -> 0.66 us
  starting transfers between devices: 9.18 us -> 0 us
    ppermute x4 -> x0, waiting for transfers between devices: 181 us -> none  [the longest x1 91.8 us: padded(): after = lax.ppermute(leading, axis, down)]
    psum x2 -> x0, waiting for transfers between devices: 133 us -> none  [the longest x1 75.4 us: shards(): mixed_rows = lax.psum(mixed_part, 'blk')]
    another operation x22 -> x0, other arithmetic: 123 us -> none  [the longest x13 66.6 us: basis_from(): lower_factor = jnp.linalg.cholesky(gram_matrix)]
    pallas_call x0 -> x1, Pallas kernels: none -> 80.7 us  [shards(): pl.pallas_call(functools.partial(kernel, nl, nb, scale), out_shape=(jax.S...]
    dot_general x16 -> x0, matrix products: 34.5 us -> none  [the longest x1 11.5 us: shards(): jnp.einsum('rbp,pk->rbk', partial_sketch, mixing, precision=highest)]
    another operation x9 -> x0, loops' own time: 20 us -> none  [the longest x1 19.9 us: shards(): partial_sketch = lax.map(leaf_sketch, jnp.arange(local_rows))]
    concatenate x1 -> x0, other arithmetic: 10.8 us -> none  [padded(): value = jnp.concatenate([before, value, after], axis=dim)]
    dynamic_slice x16 -> x0, local copies, waits for them, and re-layouts: 9.47 us -> none  [the longest x8 4.76 us: leaf_sketch(): is_live = blk_pos * near_dev + 0 < near_count[row_index]]
  transfers between devices with their start and end apart: 7 -> 0, of which waited for: 7 -> 0; matrix products, arithmetic and copies ran while one was open for 5% -> 0% of each run, Pallas kernels for 0% -> 0%
where the time goes in v1:
time: 88.3 us; the launch traced here: 88.1 us
  Pallas kernels  80.7 us (91%)
  local copies, waits for them, and re-layouts  6.73 us (8%)
    pallas_call x1, Pallas kernels, shards(): pl.pallas_call(functools.partial(kernel, nl, nb, scale), out_shape=(jax.S...  80.7 us
    unnamed x9, local copies, waits for them, and re-layouts  6.73 us

profile of v1, /device:TPU:25, one launch (start us, length us, event | category | flops | bytes accessed | tf_op | source)
XLA Modules:
  0.0 88.1 jit_solution(16772576827645117438)
XLA Ops:
  0.6 0.7 copy.9.cols
  1.4 0.7 copy.10.fcols
  2.1 1.0 %copy.11.mix = f32[512,64]{1,0:T(8,128)S(1)} copy(f32[512,64]{0,1:T(8,128)} %param.11) | data formatting | bytes 262144 | tf_op args[4]
  3.1 0.0 copy-start
  3.1 2.2 %copy-done = bf16[8,1,512,512]{3,2,1,0:T(8,128)(2,1)S(1)} copy-done((bf16[8,1,512,512]{3,2,1,0:T(8,128)(2,1)S(1)}, bf16[8,1,512,512]{3,2,1,0:T(8,128)(2,1)}, u32[]{:S(2)}) %copy-start) | copy-done | bytes 4194328
  5.3 0.0 copy-start.1
  5.3 0.7 copy-done.1
  6.0 80.7 %nested_basis.1 = (f32[8,1,64,64]{3,2,1,0:T(8,128)S(1)}, f32[8,64,64]{2,1,0:T(8,128)S(1)}) custom-call(s32[8,1]{1,0:T(8,128)S(1)} %copy.9.cols, s32[8]{0:T(128)S(1)} %copy-done.1, s32[8,1]{1,0:T(8,128)S(1)} %copy.10.fcols, bf16[8,1,512,512]{3,2,1,0:T(8,128)(2,1)S(1)} %copy-done, bf16[8,512,512]{2,1,0:T(8,128)(2,1)} %probes_hbm.1, f32[512,64]{1,0:T(8,128)S(1)} %copy.11.mix, ...), custom_call_target="tpu_custom_call" | custom-call | tf_op jit(solution)/shard_map/nested_basis/pallas_call | solution.py:357
  86.7 0.7 copy.14
  87.4 0.7 copy.15
Async XLA Ops:
  3.1 2.2 %copy-start = (bf16[8,1,512,512]{3,2,1,0:T(8,128)(2,1)S(1)}, bf16[8,1,512,512]{3,2,1,0:T(8,128)(2,1)}, u32[]{:S(2)}) copy-start(bf16[8,1,512,512]{3,2,1,0:T(8,128)(2,1)} %near_hbm.1) | copy-start | bytes 12582916
  5.3 0.7 copy-start.1

commit v2 on v1

--- a/solution.py
+++ b/solution.py
@@ -47,10 +47,10 @@
 
 def kernel(
     nl, nb, scale,
-    cols, count, fcols, near_hbm, probes_hbm, mix, far_hbm,
+    cols_hbm, count_hbm, fcols_hbm, near_hbm, probes_hbm, mix_hbm, far_hbm,
     coup, root,
-    pv, nv, fv, ywin, part, pair, sums, scat, gbuf, gleaf, ubuf, ball,
-    pin, win, h_s, h_r, f_s, f_r, p_s, p_r, r_s, r_r, g_s, g_r, gl_s, gl_r,
+    cols, count, fcols, mix, pv, nv, fv, ywin, part, pair, sums, scat, gbuf, gleaf, ubuf, ball,
+    pin, win, h_s, h_r, q_s, q_r, f_s, f_r, p_s, p_r, r_s, r_r, g_s, g_r, gl_s, gl_r,
     u_s, u_r, bm_s, bm_r, bz_s, bz_r, bl_s, bl_r, bx_s, bx_r,
 ):
     leaf = lax.axis_index("leaf")
@@ -60,7 +60,7 @@
     nz = nb // 2
     groups = nb // R
     size = pv.shape[1]
-    rank = mix.shape[1]
+    rank = mix.shape[0]
     near_dev = nv.shape[1]
     far_dev = fv.shape[1]
     core = blk % 2
@@ -68,6 +68,9 @@
     z = own // 2
     base = blk - own
     mate = blk + 1 - 2 * core
+    turn = (blk // 2) % 2
+    beside = blk + 2 - 4 * turn
+    quarter = half // 2
     pending = []
 
     def remote(src, dst, send, recv, to_leaf, to_blk):
@@ -76,18 +79,21 @@
             device_id=(to_leaf, to_blk), device_id_type=MESH,
         )
 
-    loads = []
-    for k in range(half):
-        loads.append(pltpu.make_async_copy(probes_hbm.at[2 * k + core], pv.at[2 * k + core], pin.at[k]))
-    for k in range(half):
-        i = 2 * k + 1 - core
-        loads.append(pltpu.make_async_copy(probes_hbm.at[i], pv.at[i], pin.at[half + k]))
+    order = [2 * (2 * m + turn) + core for m in range(quarter)]
+    order += [2 * (2 * m + 1 - turn) + core for m in range(quarter)]
+    order += [2 * k + 1 - core for k in range(half)]
+    mix_load = pltpu.make_async_copy(mix_hbm, mix, win.at[2])
+    mix_load.start()
+    loads = [pltpu.make_async_copy(probes_hbm.at[i], pv.at[i], pin.at[k]) for k, i in enumerate(order)]
     near_load = pltpu.make_async_copy(near_hbm, nv, win.at[0])
     far_load = pltpu.make_async_copy(far_hbm, fv, win.at[1])
-    for load in loads:
+    small_loads = [
+        pltpu.make_async_copy(cols_hbm, cols, win.at[3]),
+        pltpu.make_async_copy(count_hbm, count, win.at[4]),
+        pltpu.make_async_copy(fcols_hbm, fcols, win.at[5]),
+    ]
+    for load in loads + small_loads + [near_load, far_load]:
         load.start()
-    near_load.start()
-    far_load.start()
 
     barrier = pltpu.get_barrier_semaphore()
     for d in range(1, nl):
@@ -95,83 +101,87 @@
     for d in range(1, nb):
         pl.semaphore_signal(barrier, inc=1, device_id=(leaf, (blk + d) % nb), device_id_type=MESH)
 
-    terms = split_terms(mix[...])
+    mix_load.wait()
+    high = mix[...].astype(bf16).astype(f32)
+    terms = jnp.concatenate([high, mix[...] - high], axis=0).T.astype(bf16)
 
     def mixed(i):
         product = jnp.dot(pv[i], terms, preferred_element_type=f32)
         ywin[R + i] = split_terms(product[:, :rank] + product[:, rank:])
 
-    def up_copy(k):
-        i = 2 * k + core
-        return remote(ywin.at[R + i], ywin.at[i], h_s.at[k], h_r.at[k], (leaf + 1) % nl, blk)
-
-    def down_copy(k):
-        i = 2 * k + core
-        return remote(
-            ywin.at[R + i], ywin.at[2 * R + i], h_s.at[half + k], h_r.at[half + k], (leaf + nl - 1) % nl, blk
-        )
+    def over_leaf(side, m):
+        i = 2 * (2 * m + turn) + core
+        at = side * quarter + m
+        to = (leaf + 1) % nl if side == 0 else (leaf + nl - 1) % nl
+        return remote(ywin.at[R + i], ywin.at[2 * R * side + i], h_s.at[at], h_r.at[at], to, blk)
+
+    def over_z(side, m, whose):
+        i = 2 * R * side + 2 * (2 * m + whose) + core
+        at = side * quarter + m
+        return remote(ywin.at[i], ywin.at[i], q_s.at[at], q_r.at[at], leaf, beside)
 
     def share(side, k, parity):
         i = 2 * R * side + 2 * k + parity
-        s = side * half + k
-        return remote(ywin.at[i], ywin.at[i], f_s.at[s], f_r.at[s], leaf, mate)
+        at = side * half + k
+        return remote(ywin.at[i], ywin.at[i], f_s.at[at], f_r.at[at], leaf, mate)
 
     has_up = leaf < nl - 1
     has_down = leaf > 0
+    sends = (has_up, has_down)
+    gets = (has_down, has_up)
+    for m in range(quarter):
+        loads[m].wait()
+        mixed(order[m])
+        if m == 0:
+            pl.semaphore_wait(barrier, nl - 1 + nb - 1)
+        for side in range(2):
+
+            @pl.when(sends[side])
+            def _():
+                over_leaf(side, m).start()
+
+    for k in range(quarter, R):
+        loads[k].wait()
+        mixed(order[k])
+
+    for side in range(2):
+
+        @pl.when(jnp.logical_not(gets[side]))
+        def _():
+            ywin[2 * R * side : 2 * R * side + R] = jnp.zeros((R,) + ywin.shape[1:], bf16)
+
+    for m in range(quarter):
+        for side in range(2):
+
+            @pl.when(gets[side])
+            def _():
+                over_leaf(side, m).wait_recv()
+                over_z(side, m, turn).start()
+                share(side, 2 * m + turn, core).start()
+
+    for m in range(quarter):
+        for side in range(2):
+
+            @pl.when(gets[side])
+            def _():
+                over_z(side, m, 1 - turn).wait_recv()
+                share(side, 2 * m + 1 - turn, core).start()
+
     for k in range(half):
-        loads[k].wait()
-        mixed(2 * k + core)
-        if k == 0:
-            pl.semaphore_wait(barrier, nl - 1 + nb - 1)
-
-        @pl.when(has_up)
-        def _():
-            up_copy(k).start()
-
-        @pl.when(has_down)
-        def _():
-            down_copy(k).start()
-
-    for k in range(half):
-        loads[half + k].wait()
-        mixed(2 * k + 1 - core)
-
-    @pl.when(jnp.logical_not(has_down))
-    def _():
-        ywin[0:R] = jnp.zeros((R,) + ywin.shape[1:], bf16)
-
-    @pl.when(jnp.logical_not(has_up))
-    def _():
-        ywin[2 * R : 3 * R] = jnp.zeros((R,) + ywin.shape[1:], bf16)
-
-    for k in range(half):
-
-        @pl.when(has_down)
-        def _():
-            up_copy(k).wait_recv()
-            share(0, k, core).start()
-
-        @pl.when(has_up)
-        def _():
-            down_copy(k).wait_recv()
-            share(1, k, core).start()
-
-    for k in range(half):
-
-        @pl.when(has_down)
-        def _():
-            share(0, k, 1 - core).wait_recv()
-
-        @pl.when(has_up)
-        def _():
-            share(1, k, 1 - core).wait_recv()
-
+        for side in range(2):
+
+            @pl.when(gets[side])
+            def _():
+                share(side, k, 1 - core).wait_recv()
+
+    for load in small_loads:
+        load.wait()
     near_load.wait()
 
     def compressed(r):
         total = jnp.zeros((size, rank), f32)
         for s in range(near_dev):
-            column = jnp.clip(cols[r, s] - (leaf - 1) * R, 0, 3 * R - 1)
+            column = jnp.clip(cols[s, r] - (leaf - 1) * R, 0, 3 * R - 1)
             product = jnp.dot(nv[r, s], ywin[column], preferred_element_type=f32)
             live = blk * near_dev + s < count[r]
             total += jnp.where(live, product[:, :rank] + product[:, rank:], 0.0)
@@ -312,7 +322,7 @@
     for r in range(R):
         left = unpacked(ball[place(leaf, r % 2, r // 2)])
         for s in range(far_dev):
-            q = fcols[r, s]
+            q = fcols[s, r]
             right = unpacked(ball[place(q // R, q % 2, (q % R) // 2)])
             image = jnp.dot(fv[r, s], right, preferred_element_type=f32)
             product = lax.dot_general(
@@ -322,18 +332,24 @@
 
     for copy in pending:
         copy.wait_send()
+    for side in range(2):
+        for m in range(quarter):
+
+            @pl.when(sends[side])
+            def _():
+                over_leaf(side, m).wait_send()
+
+            @pl.when(gets[side])
+            def _():
+                over_z(side, m, turn).wait_send()
+
+        for k in range(half):
+
+            @pl.when(gets[side])
+            def _():
+                share(side, k, core).wait_send()
+
     for k in range(half):
-
-        @pl.when(has_up)
-        def _():
-            up_copy(k).wait_send()
-            share(1, k, core).wait_send()
-
-        @pl.when(has_down)
-        def _():
-            down_copy(k).wait_send()
-            share(0, k, core).wait_send()
-
         for g in range(groups):
             target = g * R + 2 * k + core
 
@@ -347,11 +363,10 @@
     R, size, width = probes.shape
     rank = mixing.shape[1]
     half, nz, groups = R // 2, nb // 2, nb // R
-    assert R % 2 == 0 and nb % R == 0 and REACH <= R and nl > 1
+    assert R % 4 == 0 and nb % R == 0 and REACH <= R and nl > 1
     dma = pltpu.SemaphoreType.DMA
     packed = (size // 2, 2 * rank)
     vmem = pl.BlockSpec(memory_space=pltpu.VMEM)
-    smem = pl.BlockSpec(memory_space=pltpu.SMEM)
     hbm = pl.BlockSpec(memory_space=pl.ANY)
     scale = math.sqrt(nl * R * rank)
     return pl.pallas_call(
@@ -360,9 +375,13 @@
             jax.ShapeDtypeStruct((R, far_tiles.shape[1], rank, rank), f32),
             jax.ShapeDtypeStruct((R, rank, rank), f32),
         ),
-        in_specs=[smem, smem, smem, hbm, hbm, vmem, hbm],
+        in_specs=[hbm] * 7,
         out_specs=(vmem, vmem),
         scratch_shapes=[
+            pltpu.SMEM(near_cols.shape[::-1], jnp.int32),
+            pltpu.SMEM(near_count.shape, jnp.int32),
+            pltpu.SMEM(far_cols.shape[::-1], jnp.int32),
+            pltpu.VMEM(mixing.shape[::-1], f32),
             pltpu.VMEM(probes.shape, bf16),
             pltpu.VMEM(near_tiles.shape, bf16),
             pltpu.VMEM(far_tiles.shape, bf16),
@@ -375,8 +394,8 @@
             pltpu.VMEM((nl, rank, rank), f32),
             pltpu.VMEM((R, rank, rank), f32),
             pltpu.VMEM((nl * R,) + packed, bf16),
-            dma((R,)), dma((2,)),
-            dma((R,)), dma((R,)), dma((R,)), dma((R,)),
+            dma((R,)), dma((6,)),
+            dma((half,)), dma((half,)), dma((half,)), dma((half,)), dma((R,)), dma((R,)),
             dma((half,)), dma((half,)),
             dma((half, groups)), dma((nz,)),
             dma((R,)), dma((R,)), dma((nl,)), dma((nl,)),
@@ -385,10 +404,10 @@
             dma((nl, half)), dma((nl, half)), dma((nl,)), dma((nl,)),
         ],
         compiler_params=pltpu.CompilerParams(
-            collective_id=0, has_side_effects=True, vmem_limit_bytes=48 * 1024 * 1024
+            collective_id=0, has_side_effects=True, vmem_limit_bytes=60 * 1024 * 1024
         ),
         name="nested_basis",
-    )(near_cols, near_count, far_cols, near_tiles, probes, mixing, far_tiles)
+    )(near_cols.T, near_count, far_cols.T, near_tiles, probes, mixing.T, far_tiles)
 
 
 def solution(mesh):

time: 88.3 us -> 78 us (0.88)
  Pallas kernels: 80.7 us -> 73.8 us
  local copies, waits for them, and re-layouts: 6.73 us -> 3.34 us
    pallas_call x1, Pallas kernels: 80.7 us -> 73.8 us  [shards(): pl.pallas_call(functools.partial(kernel, nl, nb, scale), out_shape=(jax.S...]
    unnamed x9 -> x2, local copies, waits for them, and re-layouts: 6.73 us -> 3.34 us
where the time goes in v2:
time: 78 us; the launch traced here: 77.8 us
  Pallas kernels  73.8 us (95%)
  local copies, waits for them, and re-layouts  3.34 us (4%)
    pallas_call x1, Pallas kernels, shards(): pl.pallas_call(functools.partial(kernel, nl, nb, scale), out_shape=(jax.S...  73.8 us
    unnamed x2, local copies, waits for them, and re-layouts  3.34 us

profile of v2, /device:TPU:25, one launch (start us, length us, event | category | flops | bytes accessed | tf_op | source)
XLA Modules:
  0.0 77.8 jit_solution(1461102858733974422)
XLA Ops:
  0.6 73.8 %nested_basis.1 = (f32[8,1,64,64]{3,2,1,0:T(8,128)}, f32[8,64,64]{2,1,0:T(8,128)}) custom-call(s32[1,8]{1,0:T(1,128)} %bitcast.4, s32[8]{0:T(128)} %count_hbm.1, s32[1,8]{1,0:T(1,128)} %bitcast.5, bf16[8,1,512,512]{3,2,1,0:T(8,128)(2,1)} %near_hbm.1, bf16[8,512,512]{2,1,0:T(8,128)(2,1)} %probes_hbm.1, f32[64,512]{1,0:T(8,128)} %bitcast.3, ...), custom_call_target="tpu_custom_call" | custom-call | tf_op jit(solution)/shard_map/nested_basis/pallas_call | solution.py:372
  74.5 1.7 %copy.11 = f32[8,1,64,64]{3,2,1,0:T(8,128)} copy(f32[8,1,64,64]{3,2,1,0:T(8,128)} %get-tuple-element.4) | data formatting | bytes 262144
  76.1 1.7 %copy.12 = f32[8,64,64]{2,1,0:T(8,128)} copy(f32[8,64,64]{2,1,0:T(8,128)} %get-tuple-element.5) | data formatting | bytes 262144

commit v3 on v2

--- a/solution.py
+++ b/solution.py
@@ -30,12 +30,21 @@
     done = []
     for start in range(0, rank, 8):
         index = lax.broadcasted_iota(jnp.int32, work.shape, 0)
-        for step in range(8):
+        for step in range(0, 8, 2):
             j = start + step
-            row = work[step : step + 1, :]
-            inverse = 1.0 / work[step : step + 1, j : j + 1]
-            column = work[:, j : j + 1]
-            work = work - jnp.where(index > step, column * (row * inverse), 0.0)
+            row_a = work[step : step + 1, :]
+            row_b = work[step + 1 : step + 2, :]
+            column_a = work[:, j : j + 1]
+            column_b = work[:, j + 1 : j + 2]
+            inverse_a = 1.0 / work[step : step + 1, j : j + 1]
+            cross = work[step : step + 1, j + 1 : j + 2]
+            ratio = cross * inverse_a
+            inverse_b = 1.0 / (work[step + 1 : step + 2, j + 1 : j + 2] - cross * ratio)
+            row_b = row_b - ratio * row_a
+            column_b = column_b - ratio * column_a
+            first = jnp.where(index > step, column_a * (row_a * inverse_a), 0.0)
+            second = jnp.where(index > step + 1, column_b * (row_b * inverse_b), 0.0)
+            work = work - first - second
         done.append(work[:8])
         work = work[8:] if start + 8 < rank else None
     full = jnp.concatenate(done, axis=0)
@@ -49,7 +58,7 @@
     nl, nb, scale,
     cols_hbm, count_hbm, fcols_hbm, near_hbm, probes_hbm, mix_hbm, far_hbm,
     coup, root,
-    cols, count, fcols, mix, pv, nv, fv, ywin, part, pair, sums, scat, gbuf, gleaf, ubuf, ball,
+    cols, count, fcols, mix, pv, nv, fv, ywin, part, pair, sums, scat, gbuf, gleaf, ubuf, ball, front,
     pin, win, h_s, h_r, q_s, q_r, f_s, f_r, p_s, p_r, r_s, r_r, g_s, g_r, gl_s, gl_r,
     u_s, u_r, bm_s, bm_r, bz_s, bz_r, bl_s, bl_r, bx_s, bx_r,
 ):
@@ -281,6 +290,34 @@
         remote(ball.at[at], ball.at[at], bz_s.at[d], bz_r.at[other], leaf, mate).wait_recv()
         spread(other)
 
+    for k in range(half):
+        at = place(leaf, 1 - core, k)
+        remote(ball.at[at], ball.at[at], bm_s.at[k], bm_r.at[k], leaf, mate).wait_recv()
+    far_load.wait()
+    middle = size // 2
+    for r in range(R):
+        block = ball[place(leaf, r % 2, r // 2)]
+        left = jnp.concatenate([block[:, :rank], block[:, rank:]], axis=0)
+        for s in range(far_dev):
+            image = lax.dot_general(
+                left, fv[r, s], (((0,), (0,)), ((), ())), preferred_element_type=f32
+            )
+            high = image.astype(bf16)
+            low = (image - high.astype(f32)).astype(bf16)
+            front[r, s] = jnp.concatenate(
+                [high[:, :middle], low[:, :middle], high[:, middle:], low[:, middle:]], axis=0
+            )
+
+    def relay(d):
+        s = (leaf + nl - d) % nl
+        for k in range(half):
+            at = place(s, core, k)
+            remote(ball.at[at], ball.at[at], bl_s.at[d, k], bl_r.at[s, k], s, blk).wait_recv()
+        span = pl.ds(place(s, core, 0), half)
+        copy = remote(ball.at[span], ball.at[span], bx_s.at[d], bx_r.at[s], leaf, mate)
+        copy.start()
+        pending.append(copy)
+
     for d in range(1, nl):
         s = (leaf + d) % nl
         remote(gleaf.at[s], gleaf.at[s], gl_s.at[d], gl_r.at[s], s, blk).wait_recv()
@@ -290,14 +327,7 @@
     _, root_inverse = factor(gram)
 
     for d in range(1, nl):
-        s = (leaf + nl - d) % nl
-        for k in range(half):
-            at = place(s, core, k)
-            remote(ball.at[at], ball.at[at], bl_s.at[d, k], bl_r.at[s, k], s, blk).wait_recv()
-        span = pl.ds(place(s, core, 0), half)
-        copy = remote(ball.at[span], ball.at[span], bx_s.at[d], bx_r.at[s], leaf, mate)
-        copy.start()
-        pending.append(copy)
+        relay(d)
 
     for d in range(1, R):
         j = (own + d) % R
@@ -307,28 +337,19 @@
             ubuf[r], root_inverse, (((1,), (1,)), ((), ())), precision=highest, preferred_element_type=f32
         )
 
-    for k in range(half):
-        at = place(leaf, 1 - core, k)
-        remote(ball.at[at], ball.at[at], bm_s.at[k], bm_r.at[k], leaf, mate).wait_recv()
     for d in range(1, nl):
         s = (leaf + nl - d) % nl
         span = pl.ds(place(s, 1 - core, 0), half)
         remote(ball.at[span], ball.at[span], bx_s.at[d], bx_r.at[s], leaf, mate).wait_recv()
-    far_load.wait()
-
-    def unpacked(block):
-        return jnp.concatenate([block[:, :rank], block[:, rank:]], axis=0)
 
     for r in range(R):
-        left = unpacked(ball[place(leaf, r % 2, r // 2)])
         for s in range(far_dev):
             q = fcols[s, r]
-            right = unpacked(ball[place(q // R, q % 2, (q % R) // 2)])
-            image = jnp.dot(fv[r, s], right, preferred_element_type=f32)
-            product = lax.dot_general(
-                left, split_terms(image), (((0,), (0,)), ((), ())), preferred_element_type=f32
-            )
-            coup[r, s] = product[:, :rank] + product[:, rank:]
+            block = ball[place(q // R, q % 2, (q % R) // 2)]
+            product = jnp.dot(front[r, s], block, preferred_element_type=f32)
+            upper = product[:rank] + product[rank : 2 * rank]
+            lower = product[2 * rank : 3 * rank] + product[3 * rank :]
+            coup[r, s] = upper[:, :rank] + lower[:, rank:]
 
     for copy in pending:
         copy.wait_send()
@@ -367,7 +388,7 @@
     dma = pltpu.SemaphoreType.DMA
     packed = (size // 2, 2 * rank)
     vmem = pl.BlockSpec(memory_space=pltpu.VMEM)
-    hbm = pl.BlockSpec(memory_space=pl.ANY)
+    hbm = pl.BlockSpec(memory_space=pltpu.HBM)
     scale = math.sqrt(nl * R * rank)
     return pl.pallas_call(
         functools.partial(kernel, nl, nb, scale),
@@ -394,6 +415,7 @@
             pltpu.VMEM((nl, rank, rank), f32),
             pltpu.VMEM((R, rank, rank), f32),
             pltpu.VMEM((nl * R,) + packed, bf16),
+            pltpu.VMEM((R, far_tiles.shape[1], 4 * rank, size // 2), bf16),
             dma((R,)), dma((6,)),
             dma((half,)), dma((half,)), dma((half,)), dma((half,)), dma((R,)), dma((R,)),
             dma((half,)), dma((half,)),

time: 78 us -> 75 us (0.962)
  Pallas kernels: 73.8 us -> 70.8 us
    pallas_call x1, Pallas kernels: 73.8 us -> 70.8 us  [shards(): pl.pallas_call(functools.partial(kernel, nl, nb, scale), out_shape=(jax.S...]
where the time goes in v3:
time: 75 us; the launch traced here: 74.8 us
  Pallas kernels  70.8 us (94%)
  local copies, waits for them, and re-layouts  3.34 us (4%)
    pallas_call x1, Pallas kernels, shards(): pl.pallas_call(functools.partial(kernel, nl, nb, scale), out_shape=(jax.S...  70.8 us
    unnamed x2, local copies, waits for them, and re-layouts  3.34 us

profile of v3, /device:TPU:25, one launch (start us, length us, event | category | flops | bytes accessed | tf_op | source)
XLA Modules:
  0.0 74.8 jit_solution(16220734440922269630)
XLA Ops:
  0.6 70.8 %nested_basis.1 = (f32[8,1,64,64]{3,2,1,0:T(8,128)}, f32[8,64,64]{2,1,0:T(8,128)}) custom-call(s32[1,8]{1,0:T(1,128)} %bitcast.4, s32[8]{0:T(128)} %count_hbm.1, s32[1,8]{1,0:T(1,128)} %bitcast.5, bf16[8,1,512,512]{3,2,1,0:T(8,128)(2,1)} %near_hbm.1, bf16[8,512,512]{2,1,0:T(8,128)(2,1)} %probes_hbm.1, f32[64,512]{1,0:T(8,128)} %bitcast.3, ...), custom_call_target="tpu_custom_call" | custom-call | tf_op jit(solution)/shard_map/nested_basis/pallas_call | solution.py:393
  71.4 1.7 %copy.11 = f32[8,1,64,64]{3,2,1,0:T(8,128)} copy(f32[8,1,64,64]{3,2,1,0:T(8,128)} %get-tuple-element.4) | data formatting | bytes 262144
  73.1 1.7 %copy.12 = f32[8,64,64]{2,1,0:T(8,128)} copy(f32[8,64,64]{2,1,0:T(8,128)} %get-tuple-element.5) | data formatting | bytes 262144

commit v4 on v3

--- a/solution.py
+++ b/solution.py
@@ -257,10 +257,13 @@
             copy.start()
             pending.append(copy)
 
+    def another(d):
+        return (z // 2 + d // 2) % quarter * 2 + (z + d) % 2
+
     at = place(leaf, core, z)
     ball[at] = basis.astype(bf16)
     for d in range(1, half):
-        to = (z + d) % half
+        to = another(d)
         copy = remote(ball.at[at], ball.at[at], bz_s.at[d], bz_r.at[z], leaf, base + 2 * to + core)
         copy.start()
         pending.append(copy)
@@ -284,11 +287,23 @@
         copy.start()
         pending.append(copy)
 
-    for d in range(1, half):
-        other = (z + d) % half
+    def forward(d):
+        other = another(d)
         at = place(leaf, core, other)
         remote(ball.at[at], ball.at[at], bz_s.at[d], bz_r.at[other], leaf, mate).wait_recv()
         spread(other)
+
+    forward(1)
+    for d in range(1, nl):
+        s = (leaf + d) % nl
+        remote(gleaf.at[s], gleaf.at[s], gl_s.at[d], gl_r.at[s], s, blk).wait_recv()
+    gram = gleaf[0]
+    for s in range(1, nl):
+        gram = gram + gleaf[s]
+    _, root_inverse = factor(gram)
+
+    for d in range(2, half):
+        forward(d)
 
     for k in range(half):
         at = place(leaf, 1 - core, k)
@@ -317,14 +332,6 @@
         copy = remote(ball.at[span], ball.at[span], bx_s.at[d], bx_r.at[s], leaf, mate)
         copy.start()
         pending.append(copy)
-
-    for d in range(1, nl):
-        s = (leaf + d) % nl
-        remote(gleaf.at[s], gleaf.at[s], gl_s.at[d], gl_r.at[s], s, blk).wait_recv()
-    gram = gleaf[0]
-    for s in range(1, nl):
-        gram = gram + gleaf[s]
-    _, root_inverse = factor(gram)
 
     for d in range(1, nl):
         relay(d)
@@ -426,7 +433,7 @@
             dma((nl, half)), dma((nl, half)), dma((nl,)), dma((nl,)),
         ],
         compiler_params=pltpu.CompilerParams(
-            collective_id=0, has_side_effects=True, vmem_limit_bytes=60 * 1024 * 1024
+            collective_id=0, has_side_effects=True, vmem_limit_bytes=52 * 1024 * 1024
         ),
         name="nested_basis",
     )(near_cols.T, near_count, far_cols.T, near_tiles, probes, mixing.T, far_tiles)

time: 75 us -> 78.4 us (1.045)
  Pallas kernels: 70.8 us -> 73.3 us
  local copies, waits for them, and re-layouts: 3.34 us -> 4.27 us
    pallas_call x1, Pallas kernels: 70.8 us -> 73.3 us  [shards(): pl.pallas_call(functools.partial(kernel, nl, nb, scale), out_shape=(jax.S...]
    unnamed x2 -> x10, local copies, waits for them, and re-layouts: 3.34 us -> 4.27 us
where the time goes in v4:
time: 78.4 us; the launch traced here: 78.2 us
  Pallas kernels  73.3 us (93%)
  local copies, waits for them, and re-layouts  4.27 us (5%)
    pallas_call x1, Pallas kernels, shards(): pl.pallas_call(functools.partial(kernel, nl, nb, scale), out_shape=(jax.S...  73.3 us
    unnamed x10, local copies, waits for them, and re-layouts  4.27 us

profile of v4, /device:TPU:25, one launch (start us, length us, event | category | flops | bytes accessed | tf_op | source)
XLA Modules:
  0.0 78.2 jit_solution(11194838698258577583)
XLA Ops:
  0.6 0.0 copy-start
  0.6 0.9 %copy-done = f32[512,64]{0,1:T(8,128)S(1)} copy-done((f32[512,64]{0,1:T(8,128)S(1)}, f32[512,64]{0,1:T(8,128)}, u32[]{:S(2)}) %copy-start) | copy-done | bytes 131096
  1.5 0.0 copy-start.1
  1.5 0.7 copy-done.1
  2.2 0.0 copy-start.2
  2.2 0.7 copy-done.2
  2.8 0.0 copy-start.3
  2.9 0.7 copy-done.3
  3.5 73.3 %nested_basis.1 = (f32[8,1,64,64]{3,2,1,0:T(8,128)S(1)}, f32[8,64,64]{2,1,0:T(8,128)S(1)}) custom-call(s32[1,8]{1,0:T(1,128)S(1)} %bitcast.4, s32[8]{0:T(128)S(1)} %copy-done.2, s32[1,8]{1,0:T(1,128)S(1)} %bitcast.5, bf16[8,1,512,512]{3,2,1,0:T(8,128)(2,1)} %near_hbm.1, bf16[8,512,512]{2,1,0:T(8,128)(2,1)} %probes_hbm.1, f32[64,512]{1,0:T(8,128)S(1)} %bitcast.3, ...), custom_call_target="tpu_custom_call" | custom-call | tf_op jit(solution)/shard_map/nested_basis/pallas_call | solution.py:400
  76.8 0.7 copy.11
  77.5 0.7 copy.12
Async XLA Ops:
  0.6 0.9 %copy-start = (f32[512,64]{0,1:T(8,128)S(1)}, f32[512,64]{0,1:T(8,128)}, u32[]{:S(2)}) copy-start(f32[512,64]{0,1:T(8,128)} %param.11) | copy-start | bytes 393220
  1.5 0.7 copy-start.1
  2.2 0.7 copy-start.2
  2.8 0.7 copy-start.3

commit v5 on v3

--- a/solution.py
+++ b/solution.py
@@ -257,10 +257,13 @@
             copy.start()
             pending.append(copy)
 
+    def another(d):
+        return (z // 2 + d // 2) % quarter * 2 + (z + d) % 2
+
     at = place(leaf, core, z)
     ball[at] = basis.astype(bf16)
     for d in range(1, half):
-        to = (z + d) % half
+        to = another(d)
         copy = remote(ball.at[at], ball.at[at], bz_s.at[d], bz_r.at[z], leaf, base + 2 * to + core)
         copy.start()
         pending.append(copy)
@@ -284,11 +287,15 @@
         copy.start()
         pending.append(copy)
 
-    for d in range(1, half):
-        other = (z + d) % half
+    def forward(d):
+        other = another(d)
         at = place(leaf, core, other)
         remote(ball.at[at], ball.at[at], bz_s.at[d], bz_r.at[other], leaf, mate).wait_recv()
         spread(other)
+
+    forward(1)
+    for d in range(2, half):
+        forward(d)
 
     for k in range(half):
         at = place(leaf, 1 - core, k)

time: 75 us -> 75.3 us (level); the launches traced: 74.8 us -> 74.2 us
  no operation moved by 1% of the time
where the time goes in v5:
time: 75.3 us; the launch traced here: 74.2 us
  Pallas kernels  70.3 us (93%)
  local copies, waits for them, and re-layouts  3.34 us (4%)
    pallas_call x1, Pallas kernels, shards(): pl.pallas_call(functools.partial(kernel, nl, nb, scale), out_shape=(jax.S...  70.3 us
    unnamed x2, local copies, waits for them, and re-layouts  3.34 us

profile of v5, /device:TPU:25, one launch (start us, length us, event | category | flops | bytes accessed | tf_op | source)
XLA Modules:
  0.0 74.2 jit_solution(12555867866358430378)
XLA Ops:
  0.6 70.3 %nested_basis.1 = (f32[8,1,64,64]{3,2,1,0:T(8,128)}, f32[8,64,64]{2,1,0:T(8,128)}) custom-call(s32[1,8]{1,0:T(1,128)} %bitcast.4, s32[8]{0:T(128)} %count_hbm.1, s32[1,8]{1,0:T(1,128)} %bitcast.5, bf16[8,1,512,512]{3,2,1,0:T(8,128)(2,1)} %near_hbm.1, bf16[8,512,512]{2,1,0:T(8,128)(2,1)} %probes_hbm.1, f32[64,512]{1,0:T(8,128)} %bitcast.3, ...), custom_call_target="tpu_custom_call" | custom-call | tf_op jit(solution)/shard_map/nested_basis/pallas_call | solution.py:400
  70.9 1.7 %copy.11 = f32[8,1,64,64]{3,2,1,0:T(8,128)} copy(f32[8,1,64,64]{3,2,1,0:T(8,128)} %get-tuple-element.4) | data formatting | bytes 262144
  72.6 1.7 %copy.12 = f32[8,64,64]{2,1,0:T(8,128)} copy(f32[8,64,64]{2,1,0:T(8,128)} %get-tuple-element.5) | data formatting | bytes 262144
